TPU v7x, 32 devices: a whole 2x2x4 slice. The times are simulated.
32 devices in a mesh: dp: 8 (over z, x), section: 4 (over y, core).
Axes of the slice: x: 2, y: 2, z: 4, core: 2. Of those that a mesh axis runs over, the one named last changes fastest.
Arguments:
- images_in: bfloat16 [2048, 4096], P(('dp', 'section')), may hold values from -6 to 6
- labels: int32 [2048], P(('dp', 'section')), may hold values from 0 to 9
- conv_weight: float32 [3, 2, 576, 64], P(None, None, None, 'section'), may hold values from -0.25 to 0.25
- frn_gain: float32 [3, 2, 64], replicated, may hold values from 0.25 to 1.75
- frn_bias: float32 [3, 2, 64], replicated, may hold values from -3 to 3
- head_weight: float32 [64, 10], replicated, as said below
- head_bias: float32 [10], replicated, may hold values from -4 to 4
Outputs:
- grad_conv: float32 [3, 2, 576, 64], P(None, None, None, 'section')
- grad_norm: float32 [3, 2, 2, 64], replicated
- grad_head_weight: float32 [64, 10], replicated
- grad_head_bias: float32 [10], replicated
Inputs may be any that keep to these rules, and one draw needn't show every extreme that they name: `head_weight`: the classifier's weights.
All inputs are finite; a program needn't handle non-finite values.
Results may differ from a plain program's by a relative error of at most 0.0033.
The roundings to bfloat16 on the way count: a program that leaves them out, or rounds other values in their place, can miss the bound.
Values may be sent and summed in bfloat16 or wider, within the bound.
A program may use at most 64 MiB of HBM per device.

v0:
```python
import jax
import jax.numpy as jnp
from jax import lax
from jax.sharding import PartitionSpec as P

SIDE = 8
MICRO = 8
eps = 1e-06
prior_precision = 0.5


def make_patches(maps):
    side = maps.shape[1]
    padded = jnp.pad(maps, ((0, 0), (1, 1), (1, 1), (0, 0)))
    taps = [padded[:, a : a + side, e : e + side, :] for a in range(3) for e in range(3)]
    stacked = jnp.concatenate(taps, axis=3)
    return stacked.reshape(maps.shape[0] * side * side, 9 * maps.shape[3])


def fold_patches(columns, shape):
    back = jax.vjp(make_patches, jnp.zeros(shape, jnp.float32))[1]
    return back(columns)[0]


def respond(values, gain, bias, count):
    grouped = values.reshape(count, -1, values.shape[1])
    energy = jnp.mean(grouped * grouped, axis=1, keepdims=True)
    normed = grouped * lax.rsqrt(energy + eps)
    return (gain * normed + bias).reshape(values.shape)


def swish(values):
    return values * jax.nn.sigmoid(values)


def block_forward(maps, weights, gains, biases):
    count = maps.shape[0]
    w_first = weights[0]
    w_second = weights[1]
    cols_first = make_patches(maps)
    pre_first = jnp.dot(cols_first, w_first, preferred_element_type=jnp.float32)
    hidden = swish(respond(pre_first, gains[0], biases[0], count)).astype(jnp.bfloat16)
    cols_second = make_patches(hidden.reshape(maps.shape))
    pre_second = jnp.dot(cols_second, w_second, preferred_element_type=jnp.float32)
    skip = maps.reshape(pre_second.shape).astype(jnp.float32)
    result = swish(skip + respond(pre_second, gains[1], biases[1], count)).astype(jnp.bfloat16)
    return (result.reshape(maps.shape), (cols_first, pre_first, cols_second, pre_second))


def block_backward(maps, cotangent, weights, gains, biases):
    count = maps.shape[0]
    w_first = weights[0]
    w_second = weights[1]
    saved = block_forward(maps, weights, gains, biases)[1]
    cols_first, pre_first, cols_second, pre_second = saved

    def second_part(values, skip, gain, bias):
        return swish(skip + respond(values, gain, bias, count))

    def first_part(values, gain, bias):
        return swish(respond(values, gain, bias, count))

    skip = maps.reshape(pre_second.shape).astype(jnp.float32)
    back_second = jax.vjp(second_part, pre_second, skip, gains[1], biases[1])[1]
    d_second, d_skip, dg_second, db_second = back_second(
        cotangent.reshape(pre_second.shape).astype(jnp.float32)
    )
    q_second = d_second.astype(jnp.bfloat16)
    dw_second = jnp.dot(cols_second.T, q_second, preferred_element_type=jnp.float32)
    d_hidden = fold_patches(
        jnp.dot(q_second, w_second.T, preferred_element_type=jnp.float32), maps.shape
    )
    back_first = jax.vjp(first_part, pre_first, gains[0], biases[0])[1]
    d_first, dg_first, db_first = back_first(d_hidden.reshape(pre_first.shape))
    q_first = d_first.astype(jnp.bfloat16)
    dw_first = jnp.dot(cols_first.T, q_first, preferred_element_type=jnp.float32)
    d_input = fold_patches(
        jnp.dot(q_first, w_first.T, preferred_element_type=jnp.float32), maps.shape
    )
    d_maps = (d_skip.reshape(maps.shape) + d_input).astype(jnp.bfloat16)
    d_norm = jnp.stack([jnp.stack([dg_first, db_first]), jnp.stack([dg_second, db_second])])
    return (d_maps, jnp.stack([dw_first, dw_second]), d_norm)


def head_grads(final, labels, head_w, head_b, total):
    count = final.shape[0]
    width = final.shape[3]
    pixels = final.shape[1] * final.shape[2]
    pooled = jnp.mean(final.reshape(count, pixels, width).astype(jnp.float32), axis=1)
    logits = jnp.dot(pooled, head_w, precision=lax.Precision.HIGHEST) + head_b
    top = jnp.max(logits, axis=1, keepdims=True)
    expo = jnp.exp(logits - top)
    probs = expo / jnp.sum(expo, axis=1, keepdims=True)
    onehot = (labels[:, None] == jnp.arange(head_w.shape[1])[None, :]).astype(jnp.float32)
    d_logits = (probs - onehot) / total
    d_head_w = jnp.dot(pooled.T, d_logits, precision=lax.Precision.HIGHEST)
    d_head_b = jnp.sum(d_logits, axis=0)
    d_pooled = jnp.dot(d_logits, head_w.T, precision=lax.Precision.HIGHEST) / pixels
    spread = jnp.broadcast_to(d_pooled[:, None, :], (count, pixels, width))
    return (spread.astype(jnp.bfloat16).reshape(final.shape), d_head_w, d_head_b)


def group_grads(maps, labels, weights, gains, biases, head_w, head_b, total):
    saved = []
    for index in range(weights.shape[0]):
        saved.append(maps)
        maps = block_forward(maps, weights[index], gains[index], biases[index])[0]
    cotangent, d_head_w, d_head_b = head_grads(maps, labels, head_w, head_b, total)
    conv_terms = []
    norm_terms = []
    for index in reversed(range(weights.shape[0])):
        cotangent, d_conv, d_norm = block_backward(
            saved[index], cotangent, weights[index], gains[index], biases[index]
        )
        conv_terms.insert(0, d_conv)
        norm_terms.insert(0, d_norm)
    return (jnp.stack(conv_terms), jnp.stack(norm_terms), d_head_w, d_head_b)


def accumulate(maps, labels, weights, gains, biases, head_w, head_b, total):
    width = weights.shape[3]
    initial = (
        jnp.zeros(weights.shape, jnp.float32),
        jnp.zeros((weights.shape[0], 2, 2, width), jnp.float32),
        jnp.zeros(head_w.shape, jnp.float32),
        jnp.zeros(head_b.shape, jnp.float32),
    )

    def advance(carry, item):
        terms = group_grads(item[0], item[1], weights, gains, biases, head_w, head_b, total)
        return (tuple((left + right for left, right in zip(carry, terms))), None)

    return lax.scan(advance, initial, (maps, labels))[0]


def per_device(images_in, labels, conv_weight, frn_gain, frn_bias, head_weight, head_bias):
    images = images_in.shape[0]
    width = frn_gain.shape[2]
    share = conv_weight.shape[3]
    total = images * lax.axis_size("dp") * lax.axis_size("section")
    offset = lax.axis_index("section") * share
    rounded_share = conv_weight.astype(jnp.bfloat16)
    all_conv = lax.all_gather(rounded_share, "section", axis=3, tiled=True)
    group_size = images // MICRO
    maps = images_in.reshape(MICRO, group_size, SIDE, SIDE, width)
    label_groups = labels.reshape(MICRO, group_size)
    conv_grad, norm_grad, head_w_grad, head_b_grad = accumulate(
        maps, label_groups, all_conv, frn_gain, frn_bias, head_weight, head_bias, total
    )
    summed = lax.psum(conv_grad, ("dp", "section"))
    conv_owned = lax.dynamic_slice_in_dim(summed, offset, share, 3)
    norm_sum, head_w_sum, head_b_sum = lax.psum(
        (norm_grad, head_w_grad, head_b_grad), ("dp", "section")
    )
    params = jnp.stack([frn_gain, frn_bias], axis=2)
    return (
        conv_owned + prior_precision * conv_weight,
        norm_sum + prior_precision * params,
        head_w_sum + prior_precision * head_weight,
        head_b_sum + prior_precision * head_bias,
    )


def solution(mesh):
    return jax.shard_map(
        per_device,
        mesh=mesh,
        in_specs=(
            P(("dp", "section"), None),
            P(("dp", "section")),
            P(None, None, None, "section"),
            P(),
            P(),
            P(),
            P(),
        ),
        out_specs=(P(None, None, None, "section"), P(), P(), P()),
        check_vma=False,
    )
```

profile of v0, /device:TPU:0, one launch (start us, length us, event | category | flops | bytes accessed | tf_op | source)
XLA Modules:
  0.0 816.5 jit_solution(12413973247500979296)
XLA Ops:
  9.6 8.5 %all_gather.3 = bf16[3,2,576,64]{2,3,1,0:T(8,128)(2,1)S(1)} all-gather(bf16[3,2,576,16]{2,3,1,0:T(8,128)(2,1)S(1)} %convert_element_type.386), channel_id=1, replica_groups=mesh['dp'=8,'section'=4] {'section'}, dimensions={3}, use_global_device_ids=true | all-gather | bytes 552960 | tf_op jit(solution)/shard_map/all_gather | solution.py:143
  19.2 659.0 %while.19 = (s32[]{:T(128)}, f32[3,2,576,64]{2,3,1,0:T(8,128)}, f32[3,2,2,64]{3,2,1,0:T(2,128)}, f32[64,10]{0,1:T(8,128)}, f32[10]{0:T(128)}, /*index=5*/bf16[8,...) while((s32[]{:T(128)}, f32[3,2,576,64]{2,3,1,0:T(8,128)}, ...), condition=%wide.region_29.30_spmd.clone, body=%wide.region_0.29_spmd.clone.sunk | while | flops 655682368 | bytes 99941760 | solution.py:133
  37.1 4.0 pad_slice_fusion.55
  56.0 4.0 pad_slice_fusion.57
  69.6 4.0 fusion.302
  119.4 4.0 pad_slice_fusion.55
  138.3 4.0 pad_slice_fusion.57
  152.0 4.0 fusion.302
  201.8 4.0 pad_slice_fusion.55
  220.7 4.0 pad_slice_fusion.57
  234.3 4.0 fusion.302
  284.2 4.0 pad_slice_fusion.55
  316.7 4.0 fusion.302
  366.5 4.0 pad_slice_fusion.55
  399.1 4.0 fusion.302
  448.9 4.0 pad_slice_fusion.55
  481.4 4.0 fusion.302
  531.3 4.0 pad_slice_fusion.55
  550.2 4.0 pad_slice_fusion.57
  563.8 4.0 fusion.302
  613.6 4.0 pad_slice_fusion.55
  646.1 4.0 fusion.302
  678.2 40.8 %all-reduce.51 = (f32[3,2,2,64]{3,2,1,0:T(2,128)S(1)}, f32[64,10]{0,1:T(8,128)S(1)}, f32[10]{0:T(128)S(1)}) all-reduce(f32[3,2,2,64]{3,2,1,0:T(2,128)} %get-tuple-element.157, f32[64,10]{0,1:T(8,128)} %get-tuple-element.158, f32[10]{0:T(128)} %get-tuple-element.159), channel_id=1, replica_groups=mesh['dp'=8,'section'=4] {'dp','section'}, use_global_device_ids=true, to_apply=%region_31.32 | all-reduce | flops 1418 | bytes 11344 | tf_op jit(solution)/shard_map/psum | solution.py:152
  722.8 85.1 %all-reduce.54.cloned.1.call-done = f32[3,2,576,64]{2,3,1,0:T(8,128)} async-done(((f32[3,2,576,64]{2,3,1,0:T(8,128)}), f32[3,2,576,64]{2,3,1,0:T(8,128)}) %all-reduce.54.cloned.1.call-update) | async-done | bytes 884752 | tf_op jit(solution)/shard_map/psum | solution.py:150
  (1667 shorter events, 581.6 us)
Async XLA Ops:
  7.2 800.7 %all-reduce.54.cloned.1.call-start = ((), (), s32[]{:S(2)}) async-start(), calls=%async_computation | async-start | bytes 1966080 | tf_op jit(solution)/shard_map/psum | solution.py:150
  19.2 23.2 %copy-start.5 = (bf16[3,2,576,64]{2,3,1,0:T(8,128)(2,1)}, bf16[3,2,576,64]{2,3,1,0:T(8,128)(2,1)S(1)}, u32[]{:S(2)}) copy-start(bf16[3,2,576,64]{2,3,1,0:T(8,128)(2,1)S(1)} %get-tuple-element.949) | copy-start | bytes 1327108 | tf_op jit(solution)/shard_map/while
  21.9 11.3 %copy-start.43 = (f32[64]{0:T(128)}, f32[64]{0:T(128)S(1)}, u32[]{:S(2)}) copy-start(f32[64]{0:T(128)S(1)} %get-tuple-element.737) | copy-start | bytes 772 | tf_op jit(solution)/shard_map/while
  21.9 20.9 %copy-start.40 = (f32[64]{0:T(128)}, f32[64]{0:T(128)S(1)}, u32[]{:S(2)}) copy-start(f32[64]{0:T(128)S(1)} %get-tuple-element.752) | copy-start | bytes 772 | tf_op jit(solution)/shard_map/while
  101.6 23.1 %copy-start.5 = (bf16[3,2,576,64]{2,3,1,0:T(8,128)(2,1)}, bf16[3,2,576,64]{2,3,1,0:T(8,128)(2,1)S(1)}, u32[]{:S(2)}) copy-start(bf16[3,2,576,64]{2,3,1,0:T(8,128)(2,1)S(1)} %get-tuple-element.949) | copy-start | bytes 1327108 | tf_op jit(solution)/shard_map/while
  104.2 11.3 %copy-start.43 = (f32[64]{0:T(128)}, f32[64]{0:T(128)S(1)}, u32[]{:S(2)}) copy-start(f32[64]{0:T(128)S(1)} %get-tuple-element.737) | copy-start | bytes 772 | tf_op jit(solution)/shard_map/while
  104.2 20.9 %copy-start.40 = (f32[64]{0:T(128)}, f32[64]{0:T(128)S(1)}, u32[]{:S(2)}) copy-start(f32[64]{0:T(128)S(1)} %get-tuple-element.752) | copy-start | bytes 772 | tf_op jit(solution)/shard_map/while
  184.0 23.1 %copy-start.5 = (bf16[3,2,576,64]{2,3,1,0:T(8,128)(2,1)}, bf16[3,2,576,64]{2,3,1,0:T(8,128)(2,1)S(1)}, u32[]{:S(2)}) copy-start(bf16[3,2,576,64]{2,3,1,0:T(8,128)(2,1)S(1)} %get-tuple-element.949) | copy-start | bytes 1327108 | tf_op jit(solution)/shard_map/while
  186.6 11.3 %copy-start.43 = (f32[64]{0:T(128)}, f32[64]{0:T(128)S(1)}, u32[]{:S(2)}) copy-start(f32[64]{0:T(128)S(1)} %get-tuple-element.737) | copy-start | bytes 772 | tf_op jit(solution)/shard_map/while
  186.6 20.9 %copy-start.40 = (f32[64]{0:T(128)}, f32[64]{0:T(128)S(1)}, u32[]{:S(2)}) copy-start(f32[64]{0:T(128)S(1)} %get-tuple-element.752) | copy-start | bytes 772 | tf_op jit(solution)/shard_map/while
  266.3 23.1 %copy-start.5 = (bf16[3,2,576,64]{2,3,1,0:T(8,128)(2,1)}, bf16[3,2,576,64]{2,3,1,0:T(8,128)(2,1)S(1)}, u32[]{:S(2)}) copy-start(bf16[3,2,576,64]{2,3,1,0:T(8,128)(2,1)S(1)} %get-tuple-element.949) | copy-start | bytes 1327108 | tf_op jit(solution)/shard_map/while
  268.9 11.3 %copy-start.43 = (f32[64]{0:T(128)}, f32[64]{0:T(128)S(1)}, u32[]{:S(2)}) copy-start(f32[64]{0:T(128)S(1)} %get-tuple-element.737) | copy-start | bytes 772 | tf_op jit(solution)/shard_map/while
  269.0 20.9 %copy-start.40 = (f32[64]{0:T(128)}, f32[64]{0:T(128)S(1)}, u32[]{:S(2)}) copy-start(f32[64]{0:T(128)S(1)} %get-tuple-element.752) | copy-start | bytes 772 | tf_op jit(solution)/shard_map/while
  348.7 23.1 %copy-start.5 = (bf16[3,2,576,64]{2,3,1,0:T(8,128)(2,1)}, bf16[3,2,576,64]{2,3,1,0:T(8,128)(2,1)S(1)}, u32[]{:S(2)}) copy-start(bf16[3,2,576,64]{2,3,1,0:T(8,128)(2,1)S(1)} %get-tuple-element.949) | copy-start | bytes 1327108 | tf_op jit(solution)/shard_map/while
  351.3 11.3 %copy-start.43 = (f32[64]{0:T(128)}, f32[64]{0:T(128)S(1)}, u32[]{:S(2)}) copy-start(f32[64]{0:T(128)S(1)} %get-tuple-element.737) | copy-start | bytes 772 | tf_op jit(solution)/shard_map/while
  351.3 20.9 %copy-start.40 = (f32[64]{0:T(128)}, f32[64]{0:T(128)S(1)}, u32[]{:S(2)}) copy-start(f32[64]{0:T(128)S(1)} %get-tuple-element.752) | copy-start | bytes 772 | tf_op jit(solution)/shard_map/while
  431.1 23.1 %copy-start.5 = (bf16[3,2,576,64]{2,3,1,0:T(8,128)(2,1)}, bf16[3,2,576,64]{2,3,1,0:T(8,128)(2,1)S(1)}, u32[]{:S(2)}) copy-start(bf16[3,2,576,64]{2,3,1,0:T(8,128)(2,1)S(1)} %get-tuple-element.949) | copy-start | bytes 1327108 | tf_op jit(solution)/shard_map/while
  433.7 11.3 %copy-start.43 = (f32[64]{0:T(128)}, f32[64]{0:T(128)S(1)}, u32[]{:S(2)}) copy-start(f32[64]{0:T(128)S(1)} %get-tuple-element.737) | copy-start | bytes 772 | tf_op jit(solution)/shard_map/while
  433.7 20.9 %copy-start.40 = (f32[64]{0:T(128)}, f32[64]{0:T(128)S(1)}, u32[]{:S(2)}) copy-start(f32[64]{0:T(128)S(1)} %get-tuple-element.752) | copy-start | bytes 772 | tf_op jit(solution)/shard_map/while
  513.4 23.1 %copy-start.5 = (bf16[3,2,576,64]{2,3,1,0:T(8,128)(2,1)}, bf16[3,2,576,64]{2,3,1,0:T(8,128)(2,1)S(1)}, u32[]{:S(2)}) copy-start(bf16[3,2,576,64]{2,3,1,0:T(8,128)(2,1)S(1)} %get-tuple-element.949) | copy-start | bytes 1327108 | tf_op jit(solution)/shard_map/while
  516.1 20.9 %copy-start.40 = (f32[64]{0:T(128)}, f32[64]{0:T(128)S(1)}, u32[]{:S(2)}) copy-start(f32[64]{0:T(128)S(1)} %get-tuple-element.752) | copy-start | bytes 772 | tf_op jit(solution)/shard_map/while
  595.8 23.1 %copy-start.5 = (bf16[3,2,576,64]{2,3,1,0:T(8,128)(2,1)}, bf16[3,2,576,64]{2,3,1,0:T(8,128)(2,1)S(1)}, u32[]{:S(2)}) copy-start(bf16[3,2,576,64]{2,3,1,0:T(8,128)(2,1)S(1)} %get-tuple-element.949) | copy-start | bytes 1327108 | tf_op jit(solution)/shard_map/while
  598.4 11.3 %copy-start.43 = (f32[64]{0:T(128)}, f32[64]{0:T(128)S(1)}, u32[]{:S(2)}) copy-start(f32[64]{0:T(128)S(1)} %get-tuple-element.737) | copy-start | bytes 772 | tf_op jit(solution)/shard_map/while
  598.4 20.9 %copy-start.40 = (f32[64]{0:T(128)}, f32[64]{0:T(128)S(1)}, u32[]{:S(2)}) copy-start(f32[64]{0:T(128)S(1)} %get-tuple-element.752) | copy-start | bytes 772 | tf_op jit(solution)/shard_map/while
  (378 other events, 790.3 us)
Sparse Core Ops, SparseCore 0:
  678.3 129.5 all-reduce.53
where the time goes:
time: 827 us; the launch traced here: 817 us
  local copies, waits for them, and re-layouts  424 us (51%)
  other arithmetic  151 us (18%)
  matrix products  85.6 us (10%)
  waiting for transfers between devices  85.1 us (10%)
  blocking collectives  49.3 us (6%)
  between operations  14.1 us (2%)
    concatenate x104, local copies, waits for them, and re-layouts, make_patches(): stacked = jnp.concatenate(taps, axis=3)  192 us
    slice x40, local copies, waits for them, and re-layouts, make_patches(): padded[:, a:a + side, e:e + side, :]  115 us
    psum x1, waiting for transfers between devices, per_device(): summed = lax.psum(conv_grad, ('dp', 'section'))  85.1 us
    while x800, local copies, waits for them, and re-layouts  72.5 us
    convert_element_type x40, other arithmetic, block_forward(): swish(skip + respond(pre_second, gains[1], biases[1], count))  48.6 us
    psum x1, blocking collectives, per_device(): lax.psum((norm_grad, head_w_grad, head_b_grad), ('dp', 'section'))  40.8 us
    convert_element_type x72, other arithmetic, block_forward(): swish(respond(pre_first, gains[0], biases[0], count)).astype(jnp.bfloat16)  37.2 us
    reduce_sum x48, other arithmetic, respond(): return (gain * normed + bias).reshape(values.shape)  36.8 us
  transfers between devices with their start and end apart: 1, of which 1 were waited for; matrix products, arithmetic and copies ran while one was open for 0% of the time, Pallas kernels for 0%

commit v1 on v0

--- a/solution.py
+++ b/solution.py
@@ -147,7 +147,7 @@
     conv_grad, norm_grad, head_w_grad, head_b_grad = accumulate(
         maps, label_groups, all_conv, frn_gain, frn_bias, head_weight, head_bias, total
     )
-    summed = lax.psum(conv_grad, ("dp", "section"))
+    summed = lax.psum(lax.psum(conv_grad, "section"), "dp")
     conv_owned = lax.dynamic_slice_in_dim(summed, offset, share, 3)
     norm_sum, head_w_sum, head_b_sum = lax.psum(
         (norm_grad, head_w_grad, head_b_grad), ("dp", "section")

time: 827 us -> 798 us (0.965)
  local copies, waits for them, and re-layouts: 424 us -> 404 us
  waiting for transfers between devices: 85.1 us -> 75.5 us
    slice x40, local copies, waits for them, and re-layouts: 115 us -> 100 us  [make_patches(): padded[:, a:a + side, e:e + side, :]]
    psum x1 -> x2, waiting for transfers between devices: 85.1 us -> 75.4 us  [per_device(): summed = lax.psum(lax.psum(conv_grad, 'section'), 'dp')]
    while x800 -> x928, local copies, waits for them, and re-layouts: 72.5 us -> 66.9 us
  transfers between devices with their start and end apart: 1 -> 2, of which waited for: 1 -> 2; matrix products, arithmetic and copies ran while one was open for 0% -> 0% of each run, Pallas kernels for 0% -> 0%
where the time goes in v1:
time: 798 us; the launch traced here: 788 us
  local copies, waits for them, and re-layouts  404 us (51%)
  other arithmetic  145 us (18%)
  matrix products  92.7 us (12%)
  waiting for transfers between devices  75.5 us (9%)
  blocking collectives  49 us (6%)
  between operations  14.2 us (2%)
    concatenate x104, local copies, waits for them, and re-layouts, make_patches(): stacked = jnp.concatenate(taps, axis=3)  198 us
    slice x40, local copies, waits for them, and re-layouts, make_patches(): padded[:, a:a + side, e:e + side, :]  100 us
    psum x2, waiting for transfers between devices, per_device(): summed = lax.psum(lax.psum(conv_grad, 'section'), 'dp')  75.4 us
    while x928, local copies, waits for them, and re-layouts  66.9 us
    convert_element_type x40, other arithmetic, block_forward(): swish(skip + respond(pre_second, gains[1], biases[1], count))  48.9 us
    psum x1, blocking collectives, per_device(): lax.psum((norm_grad, head_w_grad, head_b_grad), ('dp', 'section'))  40.5 us
    reduce_sum x48, other arithmetic, respond(): return (gain * normed + bias).reshape(values.shape)  36.8 us
    convert_element_type x72, other arithmetic, block_forward(): swish(respond(pre_first, gains[0], biases[0], count)).astype(jnp.bfloat16)  32.2 us
  transfers between devices with their start and end apart: 2, of which 2 were waited for; matrix products, arithmetic and copies ran while one was open for 0% of the time, Pallas kernels for 0%

profile of v1, /device:TPU:0, one launch (start us, length us, event | category | flops | bytes accessed | tf_op | source)
XLA Modules:
  0.0 788.0 jit_solution(11380797013124830302)
XLA Ops:
  9.0 8.5 %all_gather.3 = bf16[3,2,576,64]{2,3,1,0:T(8,128)(2,1)S(1)} all-gather(bf16[3,2,576,16]{2,3,1,0:T(8,128)(2,1)S(1)} %convert_element_type.386), channel_id=1, replica_groups=mesh['dp'=8,'section'=4] {'section'}, dimensions={3}, use_global_device_ids=true | all-gather | bytes 552960 | tf_op jit(solution)/shard_map/all_gather | solution.py:143
  18.6 642.3 %while.19 = (s32[]{:T(128)}, f32[3,2,576,64]{2,3,1,0:T(8,128)}, f32[3,2,2,64]{3,2,1,0:T(2,128)}, f32[64,10]{0,1:T(8,128)}, f32[10]{0:T(128)}, /*index=5*/bf16[8,...) while((s32[]{:T(128)}, f32[3,2,576,64]{2,3,1,0:T(8,128)}, ...), condition=%wide.region_29.30_spmd.clone, body=%wide.region_0.29_spmd.clone.sunk | while | flops 655682368 | bytes 101451392 | solution.py:133
  32.6 4.5 pad_slice_fusion.55
  52.1 4.0 pad_slice_fusion.57
  65.8 4.7 fusion.302
  112.9 4.5 pad_slice_fusion.55
  132.4 4.0 pad_slice_fusion.57
  146.1 4.7 fusion.302
  193.2 4.5 pad_slice_fusion.55
  212.7 4.0 pad_slice_fusion.57
  226.4 4.7 fusion.302
  273.5 4.5 pad_slice_fusion.55
  306.6 4.7 fusion.302
  353.8 4.5 pad_slice_fusion.55
  386.9 4.7 fusion.302
  434.1 4.5 pad_slice_fusion.55
  467.2 4.7 fusion.302
  514.4 4.5 pad_slice_fusion.55
  547.5 4.7 fusion.302
  594.7 4.5 pad_slice_fusion.55
  627.8 4.7 fusion.302
  661.1 36.6 %all-reduce.55.cloned.1.call-done = f32[3,2,576,64]{2,3,1,0:T(8,128)} async-done(((f32[3,2,576,64]{2,3,1,0:T(8,128)}), f32[3,2,576,64]{2,3,1,0:T(8,128)}) %all-reduce.55.cloned.1.call-update) | async-done | bytes 884752 | tf_op jit(solution)/shard_map/psum | solution.py:150
  697.7 40.5 %all-reduce.51 = (f32[3,2,2,64]{3,2,1,0:T(2,128)S(1)}, f32[64,10]{0,1:T(8,128)S(1)}, f32[10]{0:T(128)S(1)}) all-reduce(f32[3,2,2,64]{3,2,1,0:T(2,128)S(1)} %copy-done.45, f32[64,10]{0,1:T(8,128)S(1)} %copy-done.62, f32[10]{0:T(128)S(1)} %copy-done.56), channel_id=1, replica_groups=mesh['dp'=8,'section'=4] {'dp','section'}, use_global_device_ids=true, to_apply=%region_32.33 | all-reduce | flops 1418 | bytes 11344 | tf_op jit(solution)/shard_map/psum | solution.py:152
  740.7 38.8 %all-reduce.57.cloned.1.call-done = f32[3,2,576,64]{2,3,1,0:T(8,128)} async-done(((f32[3,2,576,64]{2,3,1,0:T(8,128)}), f32[3,2,576,64]{2,3,1,0:T(8,128)}) %all-reduce.57.cloned.1.call-update) | async-done | bytes 884752 | tf_op jit(solution)/shard_map/psum | solution.py:150
  (1810 shorter events, 556.1 us)
Async XLA Ops:
  7.2 690.5 %all-reduce.55.cloned.1.call-start = ((), (), s32[]{:S(2)}) async-start(), calls=%async_computation | async-start | bytes 1966080 | tf_op jit(solution)/shard_map/psum | solution.py:150
  18.6 19.9 %copy-start.5 = (bf16[3,2,576,64]{2,3,1,0:T(8,128)(2,1)}, bf16[3,2,576,64]{2,3,1,0:T(8,128)(2,1)S(1)}, u32[]{:S(2)}) copy-start(bf16[3,2,576,64]{2,3,1,0:T(8,128)(2,1)S(1)} %get-tuple-element.949) | copy-start | bytes 1327108 | tf_op jit(solution)/shard_map/while
  20.6 18.3 %copy-start.49 = (f32[64]{0:T(128)}, f32[64]{0:T(128)S(1)}, u32[]{:S(2)}) copy-start(f32[64]{0:T(128)S(1)} %get-tuple-element.752) | copy-start | bytes 772 | tf_op jit(solution)/shard_map/while
  98.9 19.9 %copy-start.5 = (bf16[3,2,576,64]{2,3,1,0:T(8,128)(2,1)}, bf16[3,2,576,64]{2,3,1,0:T(8,128)(2,1)S(1)}, u32[]{:S(2)}) copy-start(bf16[3,2,576,64]{2,3,1,0:T(8,128)(2,1)S(1)} %get-tuple-element.949) | copy-start | bytes 1327108 | tf_op jit(solution)/shard_map/while
  100.9 18.3 %copy-start.49 = (f32[64]{0:T(128)}, f32[64]{0:T(128)S(1)}, u32[]{:S(2)}) copy-start(f32[64]{0:T(128)S(1)} %get-tuple-element.752) | copy-start | bytes 772 | tf_op jit(solution)/shard_map/while
  179.2 19.9 %copy-start.5 = (bf16[3,2,576,64]{2,3,1,0:T(8,128)(2,1)}, bf16[3,2,576,64]{2,3,1,0:T(8,128)(2,1)S(1)}, u32[]{:S(2)}) copy-start(bf16[3,2,576,64]{2,3,1,0:T(8,128)(2,1)S(1)} %get-tuple-element.949) | copy-start | bytes 1327108 | tf_op jit(solution)/shard_map/while
  181.2 18.3 %copy-start.49 = (f32[64]{0:T(128)}, f32[64]{0:T(128)S(1)}, u32[]{:S(2)}) copy-start(f32[64]{0:T(128)S(1)} %get-tuple-element.752) | copy-start | bytes 772 | tf_op jit(solution)/shard_map/while
  259.5 19.9 %copy-start.5 = (bf16[3,2,576,64]{2,3,1,0:T(8,128)(2,1)}, bf16[3,2,576,64]{2,3,1,0:T(8,128)(2,1)S(1)}, u32[]{:S(2)}) copy-start(bf16[3,2,576,64]{2,3,1,0:T(8,128)(2,1)S(1)} %get-tuple-element.949) | copy-start | bytes 1327108 | tf_op jit(solution)/shard_map/while
  261.5 18.3 %copy-start.49 = (f32[64]{0:T(128)}, f32[64]{0:T(128)S(1)}, u32[]{:S(2)}) copy-start(f32[64]{0:T(128)S(1)} %get-tuple-element.752) | copy-start | bytes 772 | tf_op jit(solution)/shard_map/while
  339.8 19.9 %copy-start.5 = (bf16[3,2,576,64]{2,3,1,0:T(8,128)(2,1)}, bf16[3,2,576,64]{2,3,1,0:T(8,128)(2,1)S(1)}, u32[]{:S(2)}) copy-start(bf16[3,2,576,64]{2,3,1,0:T(8,128)(2,1)S(1)} %get-tuple-element.949) | copy-start | bytes 1327108 | tf_op jit(solution)/shard_map/while
  341.8 18.3 %copy-start.49 = (f32[64]{0:T(128)}, f32[64]{0:T(128)S(1)}, u32[]{:S(2)}) copy-start(f32[64]{0:T(128)S(1)} %get-tuple-element.752) | copy-start | bytes 772 | tf_op jit(solution)/shard_map/while
  420.1 19.9 %copy-start.5 = (bf16[3,2,576,64]{2,3,1,0:T(8,128)(2,1)}, bf16[3,2,576,64]{2,3,1,0:T(8,128)(2,1)S(1)}, u32[]{:S(2)}) copy-start(bf16[3,2,576,64]{2,3,1,0:T(8,128)(2,1)S(1)} %get-tuple-element.949) | copy-start | bytes 1327108 | tf_op jit(solution)/shard_map/while
  422.0 18.3 %copy-start.49 = (f32[64]{0:T(128)}, f32[64]{0:T(128)S(1)}, u32[]{:S(2)}) copy-start(f32[64]{0:T(128)S(1)} %get-tuple-element.752) | copy-start | bytes 772 | tf_op jit(solution)/shard_map/while
  500.4 19.9 %copy-start.5 = (bf16[3,2,576,64]{2,3,1,0:T(8,128)(2,1)}, bf16[3,2,576,64]{2,3,1,0:T(8,128)(2,1)S(1)}, u32[]{:S(2)}) copy-start(bf16[3,2,576,64]{2,3,1,0:T(8,128)(2,1)S(1)} %get-tuple-element.949) | copy-start | bytes 1327108 | tf_op jit(solution)/shard_map/while
  502.3 18.3 %copy-start.49 = (f32[64]{0:T(128)}, f32[64]{0:T(128)S(1)}, u32[]{:S(2)}) copy-start(f32[64]{0:T(128)S(1)} %get-tuple-element.752) | copy-start | bytes 772 | tf_op jit(solution)/shard_map/while
  580.7 19.9 %copy-start.5 = (bf16[3,2,576,64]{2,3,1,0:T(8,128)(2,1)}, bf16[3,2,576,64]{2,3,1,0:T(8,128)(2,1)S(1)}, u32[]{:S(2)}) copy-start(bf16[3,2,576,64]{2,3,1,0:T(8,128)(2,1)S(1)} %get-tuple-element.949) | copy-start | bytes 1327108 | tf_op jit(solution)/shard_map/while
  582.6 18.3 %copy-start.49 = (f32[64]{0:T(128)}, f32[64]{0:T(128)S(1)}, u32[]{:S(2)}) copy-start(f32[64]{0:T(128)S(1)} %get-tuple-element.752) | copy-start | bytes 772 | tf_op jit(solution)/shard_map/while
  660.9 36.8 %copy-start.45 = (f32[3,2,2,64]{3,2,1,0:T(2,128)S(1)}, f32[3,2,2,64]{3,2,1,0:T(2,128)}, u32[]{:S(2)}) copy-start(f32[3,2,2,64]{3,2,1,0:T(2,128)} %get-tuple-element.157) | copy-start | bytes 9220
  660.9 36.8 %copy-start.56 = (f32[10]{0:T(128)S(1)}, f32[10]{0:T(128)}, u32[]{:S(2)}) copy-start(f32[10]{0:T(128)} %get-tuple-element.159) | copy-start | bytes 124
  660.9 36.8 %copy-start.62 = (f32[64,10]{0,1:T(8,128)S(1)}, f32[64,10]{0,1:T(8,128)}, u32[]{:S(2)}) copy-start(f32[64,10]{0,1:T(8,128)} %get-tuple-element.158) | copy-start | bytes 7684
  661.0 77.3 %copy-start.58 = (f32[10]{0:T(128)S(1)}, f32[10]{0:T(128)}, u32[]{:S(2)}) copy-start(f32[10]{0:T(128)} %get-tuple-element.965) | copy-start | bytes 124
  661.0 79.1 %copy-start.42 = (f32[64,10]{0,1:T(8,128)S(1)}, f32[64,10]{0,1:T(8,128)}, u32[]{:S(2)}) copy-start(f32[64,10]{0,1:T(8,128)} %get-tuple-element.963) | copy-start | bytes 7684
  661.0 118.6 %copy-start.27 = (f32[3,2,576,16]{2,3,1,0:T(8,128)S(1)}, f32[3,2,576,16]{2,3,1,0:T(8,128)}, u32[]{:S(2)}) copy-start(f32[3,2,576,16]{2,3,1,0:T(8,128)} %param.11) | copy-start | bytes 663556
  661.0 118.5 %all-reduce.57.cloned.1.call-start = ((), (), s32[]{:S(2)}) async-start(), calls=%async_computation.1 | async-start | bytes 1966080 | tf_op jit(solution)/shard_map/psum | solution.py:150
  (449 other events, 987.3 us)
Sparse Core Ops, SparseCore 0:
  661.1 36.5 all-reduce.54
  701.5 77.9 all-reduce.56
